TPU v7x, 32 devices: a whole 2x2x4 slice. The times are simulated.
32 devices in a mesh: req: 16 (over z, x, core), exp: 2 (over y).
Axes of the slice: x: 2, y: 2, z: 4, core: 2. Of those that a mesh axis runs over, the one named last changes fastest.
Arguments:
- residual: bfloat16 [32, 64, 2560], P(('exp', 'req')), may hold values from -40 to 40
- queries: bfloat16 [32, 64, 2560], P(('exp', 'req')), may hold values from -95 to 95
- fresh_kv: bfloat16 [32, 64, 1024], P(('exp', 'req')), may hold values from -5.1 to 5.1
- cache_key_value: bfloat16 [2048, 32, 1024], P('req', 'exp'), may hold values from -5 to 5
- lengths: int32 [32], P(('exp', 'req')), may hold values from 256 to 2048, as said below
- expert_ids: int32 [32, 64, 6], P(('exp', 'req')), may hold values from 0 to 15, all different within a row; in each aligned block of 64 rows (0 to 63, 64 to 127, ..., all dimensions but the last counted through in order) at most 30 rows name the same one
- router_w: float32 [32, 64, 6], P(('exp', 'req')), may hold values from 0.2 to 1
- norm_gain: float32 [2560], replicated, may hold values from 0.5 to 1.5
- gate_w: bfloat16 [16, 2560, 1536], P('req', None, 'exp'), may hold values from -0.125 to 0.125
- up_w: bfloat16 [16, 2560, 1536], P('req', None, 'exp'), may hold values from -0.125 to 0.125
- down_w: bfloat16 [16, 2560, 1536], P('req', None, 'exp'), may hold values from -0.15625 to 0.15625
Outputs:
- mixed: bfloat16 [32, 64, 2560], P(('exp', 'req'))
Inputs may be any that keep to these rules, and one draw needn't show every extreme that they name: `expert_ids`: each token names 6 different experts. Among the tokens of one request no expert is named more than 30 times, and in every draw some expert is named exactly 30 times by one request. `lengths`: some request has exactly 2048 cached positions.
All inputs are finite; a program needn't handle non-finite values.
Results may differ from a plain program's by a relative error of at most 0.006.
Values may be sent and summed in bfloat16 or wider, within the bound.
A program may use at most 128 MiB of HBM per device.

v0:
```python
import math

import jax
import jax.numpy as jnp
from jax import lax
from jax.sharding import PartitionSpec as P

QUERY_HEADS = 20
KEY_VALUE_HEADS = 4
HEAD_SIZE = 128


def block_terms(batch_rows, gate_part, up_part, down_part, block):
    width = gate_part.shape[0]
    count = gate_part.shape[1] // block
    gate_blocks = gate_part.reshape(width, count, block)
    up_blocks = up_part.reshape(width, count, block)
    down_blocks = down_part.reshape(width, count, block)
    gate_val = jnp.einsum(
        "rd,dkf->krf", batch_rows, gate_blocks, preferred_element_type=jnp.float32
    )
    up_val = jnp.einsum("rd,dkf->krf", batch_rows, up_blocks, preferred_element_type=jnp.float32)
    active = (jax.nn.silu(gate_val) * up_val).astype(jnp.bfloat16)
    partial_value = jnp.einsum(
        "krf,dkf->krd", active, down_blocks, preferred_element_type=jnp.float32
    ).astype(jnp.bfloat16)
    return jnp.sum(partial_value.astype(jnp.float32), axis=0)


def per_device(
    residual,
    queries,
    fresh_kv,
    cache_key_value,
    lengths,
    expert_ids,
    router_w,
    norm_gain,
    gate_w,
    up_w,
    down_w,
):
    pages = lax.all_to_all(cache_key_value, "req", split_axis=1, concat_axis=0, tiled=True)
    token_count = residual.shape[1]
    width = residual.shape[2]
    group_size = QUERY_HEADS // KEY_VALUE_HEADS
    key_value_keys = KEY_VALUE_HEADS * HEAD_SIZE
    grouped_queries = queries[0].reshape(token_count, KEY_VALUE_HEADS, group_size, HEAD_SIZE)
    cached_entries = pages[:, 0, :]
    recent_entries = fresh_kv[0]
    stored_keys = cached_entries[:, :key_value_keys].reshape(-1, KEY_VALUE_HEADS, HEAD_SIZE)
    stored_values = cached_entries[:, key_value_keys:].reshape(-1, KEY_VALUE_HEADS, HEAD_SIZE)
    recent_keys = recent_entries[:, :key_value_keys].reshape(-1, KEY_VALUE_HEADS, HEAD_SIZE)
    recent_values = recent_entries[:, key_value_keys:].reshape(-1, KEY_VALUE_HEADS, HEAD_SIZE)
    scale = 1.0 / math.sqrt(HEAD_SIZE)
    score_old = (
        jnp.einsum(
            "tgjd,pgd->gjtp", grouped_queries, stored_keys, preferred_element_type=jnp.float32
        )
        * scale
    )
    score_new = (
        jnp.einsum(
            "tgjd,cgd->gjtc", grouped_queries, recent_keys, preferred_element_type=jnp.float32
        )
        * scale
    )
    length = lengths[0]
    score_old = jnp.where(jnp.arange(cached_entries.shape[0]) < length, score_old, -jnp.inf)
    token_pos = jnp.arange(token_count)
    score_new = jnp.where(token_pos[None, :] <= token_pos[:, None], score_new, -jnp.inf)
    peak = jnp.maximum(jnp.max(score_old, axis=-1), jnp.max(score_new, axis=-1))[..., None]
    raised_old = jnp.exp(score_old - peak)
    raised_new = jnp.exp(score_new - peak)
    summed = jnp.sum(raised_old, axis=-1, keepdims=True) + jnp.sum(
        raised_new, axis=-1, keepdims=True
    )
    probs_old = (raised_old / summed).astype(jnp.bfloat16)
    probs_new = (raised_new / summed).astype(jnp.bfloat16)
    attended = jnp.einsum(
        "gjtp,pgd->tgjd", probs_old, stored_values, preferred_element_type=jnp.float32
    )
    attended = attended + jnp.einsum(
        "gjtc,cgd->tgjd", probs_new, recent_values, preferred_element_type=jnp.float32
    )
    attended = attended.reshape(token_count, width).astype(jnp.bfloat16)
    hidden = residual[0].astype(jnp.float32) + attended.astype(jnp.float32)
    normed = (
        hidden * lax.rsqrt(jnp.mean(hidden * hidden, axis=-1, keepdims=True) + 1e-06) * norm_gain
    ).astype(jnp.bfloat16)
    experts = lax.axis_size("req") * gate_w.shape[0]
    top_k = expert_ids.shape[2]
    capacity = min(token_count, 5 * token_count * top_k // (4 * experts))
    flat_ids = expert_ids[0].reshape(-1)
    one_hot = (flat_ids[:, None] == jnp.arange(experts, dtype=jnp.int32)[None, :]).astype(jnp.int32)
    slot_of = jnp.sum((jnp.cumsum(one_hot, axis=0) - 1) * one_hot, axis=1)
    repeated = jnp.repeat(normed, top_k, axis=0)
    outbound = (
        jnp.zeros((experts, capacity, width), jnp.bfloat16).at[flat_ids, slot_of].set(repeated)
    )
    inbound = lax.all_to_all(outbound, "req", split_axis=0, concat_axis=0, tiled=True)
    batch_rows = inbound.reshape(-1, width)
    block = gate_w.shape[2]
    produced = block_terms(
        batch_rows,
        lax.all_gather(gate_w, "exp", axis=2, tiled=True)[0],
        lax.all_gather(up_w, "exp", axis=2, tiled=True)[0],
        lax.all_gather(down_w, "exp", axis=2, tiled=True)[0],
        block,
    )
    produced = produced.astype(jnp.bfloat16).reshape(inbound.shape)
    returned = lax.all_to_all(produced, "req", split_axis=0, concat_axis=0, tiled=True)
    picked = returned[flat_ids, slot_of].reshape(token_count, top_k, width)
    routed = jnp.einsum("tk,tkd->td", router_w[0], picked, preferred_element_type=jnp.float32)
    mixed = (hidden + routed).astype(jnp.bfloat16)
    return mixed[None]


def solution(mesh):
    in_specs = (
        P(("exp", "req"), None, None),
        P(("exp", "req"), None, None),
        P(("exp", "req"), None, None),
        P("req", "exp", None),
        P(("exp", "req")),
        P(("exp", "req"), None, None),
        P(("exp", "req"), None, None),
        P(),
        P("req", None, "exp"),
        P("req", None, "exp"),
        P("req", None, "exp"),
    )
    out_specs = P(("exp", "req"), None, None)
    return jax.shard_map(
        per_device, mesh=mesh, in_specs=in_specs, out_specs=out_specs, check_vma=False
    )
```

profile of v0, /device:TPU:11, one launch (start us, length us, event | category | flops | bytes accessed | tf_op | source)
XLA Modules:
  0.0 423.0 jit_solution(14639481857845053867)
XLA Ops:
  6.5 6.3 %copy.76 = bf16[1,2560,768]{1,2,0:T(8,128)(2,1)} copy(bf16[1,2560,768]{2,1,0:T(8,128)(2,1)} %param.20) | data formatting | bytes 7864320 | tf_op args[9]
  12.9 6.4 %copy.74 = bf16[1,2560,768]{1,2,0:T(8,128)(2,1)} copy(bf16[1,2560,768]{2,1,0:T(8,128)(2,1)} %param.19) | data formatting | bytes 7864320 | tf_op args[8]
  19.3 7.1 %copy.58 = bf16[128,16,1024]{2,0,1:T(8,128)(2,1)} copy(bf16[128,16,1024]{2,1,0:T(8,128)(2,1)} %param.14) | data formatting | bytes 8388608 | tf_op args[3]
  26.4 6.7 %all-to-all-start = ((bf16[128,16,1024]{2,0,1:T(8,128)(2,1)}), bf16[128,16,1024]{2,0,1:T(8,128)(2,1)}, u32[]{:S(2)}, u32[]{:S(2)}) async-start(bf16[128,16,1024]{2,0,1:T(8,128)(2,1)} %copy.58), calls=%async_computation | async-start | bytes 8388608 | tf_op jit(solution)/shard_map/all_to_all | solution.py:43
  33.3 6.3 %copy.78 = bf16[1,2560,768]{1,2,0:T(8,128)(2,1)} copy(bf16[1,2560,768]{2,1,0:T(8,128)(2,1)} %param.21) | data formatting | bytes 7864320 | tf_op args[10]
  39.6 0.7 copy-done.8
  42.0 0.9 reduce-window.6
  43.2 0.4 fusion.35
  43.7 81.9 %all-to-all-done = bf16[128,16,1024]{2,0,1:T(8,128)(2,1)} async-done(((bf16[128,16,1024]{2,0,1:T(8,128)(2,1)}), bf16[128,16,1024]{2,0,1:T(8,128)(2,1)}, u32[]{:S(2)}, u32[]{:S(2)}) %all-to-all-start) | async-done | bytes 4194336 | tf_op jit(solution)/shard_map/all_to_all | solution.py:43
  125.6 5.0 %fusion.33 = (bf16[2048,512]{1,0:T(8,128)(2,1)}, bf16[2048,512]{1,0:T(8,128)(2,1)}) fusion(bf16[2048,1024]{1,0:T(8,128)(2,1)} %bitcast.4), kind=kLoop, calls=%fused_computation.64 | loop fusion | bytes 8388608 | tf_op jit(solution)/shard_map/slice | solution.py:51
  130.6 3.0 copy.59
  133.6 1.8 bitcast_reduce_fusion
  135.4 2.2 fusion.1
  137.6 2.0 copy-done
  139.8 2.5 copy.64
  142.2 6.1 %fusion.2 = f32[4,5,64,128]{3,2,1,0:T(8,128)S(1)} fusion(bf16[2048,4,128,1]{0,2,3,1:T(8,128)(2,1)} %bitcast.104, f32[4,2048,64,5]{1,2,3,0:T(8,128)} %copy-done, f32[4,5,64]{2,1,0:T(8,128)S(1)} %add.58, f32[4,5,64]{2,1,0:T(8,128)S(1)} %max.7, pred[2048]{0:T(1024)(128)(4,1)S(1)} %iota_compare_fusion.3), kind=kOutput, calls=%fused_computation.9 | convolution fusion | flops 684195840 | bytes 13250560 | tf_op jit(solution)/shard_map/gjtp,pgd->tgjd/dot_general | solution.py:80
  149.9 2.1 reshape.130
  152.3 59.3 %scatter_fusion = bf16[16,30,2560]{2,0,1:T(8,128)(2,1)S(1)} fusion(bf16[16,30,2560]{2,0,1:T(8,128)(2,1)S(1)} %broadcast_in_dim.41, s32[384]{0:T(512)S(1)} %get-tuple-element.6, bf16[384,2560]{1,0:T(8,128)(2,1)} %reshape.130), kind=kCustom, calls=%fused_computation.1 | custom fusion | bytes 5901312 | tf_op jit(solution)/shard_map/scatter | solution.py:99
  211.6 1.4 copy.73
  212.9 63.7 %all_to_all.25 = bf16[16,30,2560]{2,1,0:T(8,128)(2,1)S(1)} all-to-all(bf16[16,30,2560]{2,1,0:T(8,128)(2,1)S(1)} %copy.73), channel_id=1, replica_groups=mesh['req'=16,'exp'=2] {'req'}, dimensions={0} | all-to-all | bytes 4915200 | tf_op jit(solution)/shard_map/all_to_all | solution.py:101
  276.7 2.2 reshape.138
  278.9 9.7 %fusion.36 = f32[480,2,768]{2,0,1:T(8,128)} fusion(bf16[480,2560,1]{1,0,2:T(8,128)(2,1)} %reshape.138, bf16[2560,2,768]{0,2,1:T(8,128)(2,1)} %bitcast.110), kind=kOutput, calls=%fused_computation.67 | convolution fusion | flops 3774873600 | bytes 13271040 | tf_op jit(solution)/shard_map/rd,dkf->krf/dot_general | solution.py:22
  288.6 23.1 %all-gather.8.cloned.1.call-done = bf16[1,2560,1536]{1,2,0:T(8,128)(2,1)} async-done(((bf16[1,2560,768]{1,2,0:T(8,128)(2,1)}), bf16[1,2560,1536]{1,2,0:T(8,128)(2,1)}) %all-gather.8.cloned.1.call-update) | async-done | bytes 7864336 | tf_op jit(solution)/shard_map/all_gather | solution.py:108
  311.7 16.3 %fusion.7 = bf16[480,2560]{1,0:T(8,128)(2,1)} fusion(bf16[2560,2,768]{0,2,1:T(8,128)(2,1)} %bitcast.112, f32[480,2,768]{2,0,1:T(8,128)} %fusion.36, bf16[480,2560,1]{1,0,2:T(8,128)(2,1)S(1)} %copy-done.4, bf16[2560,2,768]{0,2,1:T(8,128)(2,1)} %bitcast.111), kind=kOutput, calls=%fused_computation.17 | convolution fusion | flops 7557857280 | bytes 23592960 | tf_op jit(solution)/shard_map/krf,dkf->krd/dot_general | solution.py:24
  328.0 4.2 reshape.118
  332.2 6.5 %all-to-all-start.2 = ((bf16[16,30,2560]{2,1,0:T(8,128)(2,1)}), bf16[16,30,2560]{2,1,0:T(8,128)(2,1)}, u32[]{:S(2)}, u32[]{:S(2)}) async-start(bf16[16,30,2560]{2,1,0:T(8,128)(2,1)} %reshape.118), calls=%async_computation.2 | async-start | bytes 5242880 | tf_op jit(solution)/shard_map/all_to_all | solution.py:112
  338.8 58.7 %all-to-all-done.2 = bf16[16,30,2560]{2,1,0:T(8,128)(2,1)} async-done(((bf16[16,30,2560]{2,1,0:T(8,128)(2,1)}), bf16[16,30,2560]{2,1,0:T(8,128)(2,1)}, u32[]{:S(2)}, u32[]{:S(2)}) %all-to-all-start.2) | async-done | bytes 2457632 | tf_op jit(solution)/shard_map/all_to_all | solution.py:112
  397.5 3.1 copy.80
  400.6 11.5 %gather_fusion = bf16[384,2560]{1,0:T(8,128)(2,1)} fusion(bf16[16,30,2560]{2,0,1:T(8,128)(2,1)S(1)} %copy.80, s32[384]{0:T(512)S(1)} %get-tuple-element.5), kind=kCustom, calls=%fused_computation | custom fusion | bytes 3935232 | tf_op jit(solution)/shard_map/gather | solution.py:113
  412.0 2.6 reshape.119
  414.6 0.8 fusion.37
  415.6 0.8 fusion.16
  (53 shorter events, 3.9 us)
Async XLA Ops:
  6.5 272.4 %all-gather.6.cloned.1.call-start = ((), (), s32[]{:S(2)}) async-start(), calls=%async_computation.4 | async-start | bytes 11796480 | tf_op jit(solution)/shard_map/all_gather | solution.py:107
  12.9 275.7 %all-gather.4.cloned.1.call-start = ((), (), s32[]{:S(2)}) async-start(), calls=%async_computation.3 | async-start | bytes 11796480 | tf_op jit(solution)/shard_map/all_gather | solution.py:106
  26.4 99.1 %all-to-all-start = ((bf16[128,16,1024]{2,0,1:T(8,128)(2,1)}), bf16[128,16,1024]{2,0,1:T(8,128)(2,1)}, u32[]{:S(2)}, u32[]{:S(2)}) async-start(bf16[128,16,1024]{2,0,1:T(8,128)(2,1)} %copy.58), calls=%async_computation | async-start | bytes 8388608 | tf_op jit(solution)/shard_map/all_to_all | solution.py:43
  33.1 278.6 %all-gather.8.cloned.1.call-start = ((), (), s32[]{:S(2)}) async-start(), calls=%async_computation.5 | async-start | bytes 11796480 | tf_op jit(solution)/shard_map/all_gather | solution.py:108
  39.6 0.7 copy-start.8
  39.6 1.9 copy-start.5
  39.6 2.3 copy-start.6
  135.4 4.2 %copy-start = (f32[4,2048,64,5]{1,2,3,0:T(8,128)}, f32[4,2048,64,5]{1,2,3,0:T(8,128)S(1)}, u32[]{:S(2)}) copy-start(f32[4,2048,64,5]{1,2,3,0:T(8,128)S(1)} %get-tuple-element.12) | copy-start | bytes 31457284
  135.4 4.4 %copy-start.1 = (bf16[2048,512]{1,0:T(8,128)(2,1)S(1)}, bf16[2048,512]{1,0:T(8,128)(2,1)}, u32[]{:S(2)}) copy-start(bf16[2048,512]{1,0:T(8,128)(2,1)} %get-tuple-element.8) | copy-start | bytes 6291460
  148.3 1.0 copy-start.2
  148.3 1.2 copy-start.7
  278.9 32.7 %copy-start.4 = (bf16[480,2560,1]{1,0,2:T(8,128)(2,1)S(1)}, bf16[480,2560,1]{1,0,2:T(8,128)(2,1)}, u32[]{:S(2)}) copy-start(bf16[480,2560,1]{1,0,2:T(8,128)(2,1)} %reshape.138) | copy-start | bytes 7372804
  332.2 6.5 %copy-start.9 = (f32[1,64,6]{1,0,2:T(1,128)S(1)}, f32[1,64,6]{1,0,2:T(1,128)}, u32[]{:S(2)}) copy-start(f32[1,64,6]{1,0,2:T(1,128)} %param.17) | copy-start | bytes 4612
  332.2 65.3 %all-to-all-start.2 = ((bf16[16,30,2560]{2,1,0:T(8,128)(2,1)}), bf16[16,30,2560]{2,1,0:T(8,128)(2,1)}, u32[]{:S(2)}, u32[]{:S(2)}) async-start(bf16[16,30,2560]{2,1,0:T(8,128)(2,1)} %reshape.118), calls=%async_computation.2 | async-start | bytes 5242880 | tf_op jit(solution)/shard_map/all_to_all | solution.py:112
  414.6 1.0 copy-start.3
Sparse Core Ops, SparseCore 0:
  13.0 99.2 all-gather.5
  113.8 98.0 all-gather.3
  213.5 98.0 all-gather.7
where the time goes:
time: 425 us; the launch traced here: 423 us
  waiting for transfers between devices  164 us (39%)
  local copies, waits for them, and re-layouts  128 us (30%)
  blocking collectives  63.7 us (15%)
  matrix products  35.4 us (8%)
  between operations  14 us (3%)
  starting transfers between devices  13.4 us (3%)
  other arithmetic  4.6 us (1%)
    all_to_all x1, waiting for transfers between devices, per_device(): lax.all_to_all(cache_key_value, 'req', split_axis=1, concat_axis=0, tiled...  81.9 us
    all_to_all x1, blocking collectives, per_device(): lax.all_to_all(outbound, 'req', split_axis=0, concat_axis=0, tiled=True)  63.7 us
    scatter x2, local copies, waits for them, and re-layouts, per_device(): jnp.zeros((experts, capacity, width), jnp.bfloat16).at[flat_ids, slot_of]  60.7 us
    all_to_all x1, waiting for transfers between devices, per_device(): lax.all_to_all(produced, 'req', split_axis=0, concat_axis=0, tiled=True)  58.7 us
    unnamed x25, local copies, waits for them, and re-layouts  29 us
    all_gather x1, waiting for transfers between devices, per_device(): lax.all_gather(down_w, 'exp', axis=2, tiled=True)[0]  23.1 us
    dot_general x1, matrix products, block_terms(): jnp.einsum('krf,dkf->krd', active, down_blocks, preferred_element_type=jn...  16.3 us
    gather x1, local copies, waits for them, and re-layouts, per_device(): picked = returned[flat_ids, slot_of].reshape(token_count, top_k, width)  11.5 us
  transfers between devices with their start and end apart: 5, of which 3 were waited for; matrix products, arithmetic and copies ran while one was open for 28% of the time, Pallas kernels for 0%

commit v1 on v0

--- a/solution.py
+++ b/solution.py
@@ -10,19 +10,14 @@
 HEAD_SIZE = 128
 
 
-def block_terms(batch_rows, gate_part, up_part, down_part, block):
-    width = gate_part.shape[0]
-    count = gate_part.shape[1] // block
-    gate_blocks = gate_part.reshape(width, count, block)
-    up_blocks = up_part.reshape(width, count, block)
-    down_blocks = down_part.reshape(width, count, block)
+def block_terms(batch_rows, gate_blocks, up_blocks, down_blocks):
     gate_val = jnp.einsum(
-        "rd,dkf->krf", batch_rows, gate_blocks, preferred_element_type=jnp.float32
+        "rd,kdf->krf", batch_rows, gate_blocks, preferred_element_type=jnp.float32
     )
-    up_val = jnp.einsum("rd,dkf->krf", batch_rows, up_blocks, preferred_element_type=jnp.float32)
+    up_val = jnp.einsum("rd,kdf->krf", batch_rows, up_blocks, preferred_element_type=jnp.float32)
     active = (jax.nn.silu(gate_val) * up_val).astype(jnp.bfloat16)
     partial_value = jnp.einsum(
-        "krf,dkf->krd", active, down_blocks, preferred_element_type=jnp.float32
+        "krf,kdf->krd", active, down_blocks, preferred_element_type=jnp.float32
     ).astype(jnp.bfloat16)
     return jnp.sum(partial_value.astype(jnp.float32), axis=0)
 
@@ -91,27 +86,34 @@
     experts = lax.axis_size("req") * gate_w.shape[0]
     top_k = expert_ids.shape[2]
     capacity = min(token_count, 5 * token_count * top_k // (4 * experts))
-    flat_ids = expert_ids[0].reshape(-1)
-    one_hot = (flat_ids[:, None] == jnp.arange(experts, dtype=jnp.int32)[None, :]).astype(jnp.int32)
-    slot_of = jnp.sum((jnp.cumsum(one_hot, axis=0) - 1) * one_hot, axis=1)
-    repeated = jnp.repeat(normed, top_k, axis=0)
-    outbound = (
-        jnp.zeros((experts, capacity, width), jnp.bfloat16).at[flat_ids, slot_of].set(repeated)
+    chosen = expert_ids[0][:, :, None] == jnp.arange(experts, dtype=jnp.int32)
+    named = jnp.any(chosen, axis=1)
+    weight = jnp.sum(jnp.where(chosen, router_w[0][:, :, None], 0.0), axis=1)
+    place = jnp.cumsum(named.astype(jnp.int32), axis=0) - 1
+    slots = jnp.arange(capacity, dtype=jnp.int32)
+    held = named[:, :, None] & (place[:, :, None] == slots)
+    held = held.reshape(token_count, experts * capacity)
+    outbound = jnp.einsum(
+        "ts,td->sd", held.astype(jnp.bfloat16), normed, preferred_element_type=jnp.float32
     )
+    outbound = outbound.astype(jnp.bfloat16).reshape(experts, capacity, width)
     inbound = lax.all_to_all(outbound, "req", split_axis=0, concat_axis=0, tiled=True)
     batch_rows = inbound.reshape(-1, width)
-    block = gate_w.shape[2]
     produced = block_terms(
         batch_rows,
-        lax.all_gather(gate_w, "exp", axis=2, tiled=True)[0],
-        lax.all_gather(up_w, "exp", axis=2, tiled=True)[0],
-        lax.all_gather(down_w, "exp", axis=2, tiled=True)[0],
-        block,
+        lax.all_gather(gate_w[0], "exp", axis=0),
+        lax.all_gather(up_w[0], "exp", axis=0),
+        lax.all_gather(down_w[0], "exp", axis=0),
     )
     produced = produced.astype(jnp.bfloat16).reshape(inbound.shape)
     returned = lax.all_to_all(produced, "req", split_axis=0, concat_axis=0, tiled=True)
-    picked = returned[flat_ids, slot_of].reshape(token_count, top_k, width)
-    routed = jnp.einsum("tk,tkd->td", router_w[0], picked, preferred_element_type=jnp.float32)
+    returned = returned.reshape(experts * capacity, width)
+    scaled = jnp.where(held, jnp.repeat(weight, capacity, axis=1), 0.0)
+    upper = lax.reduce_precision(scaled, 8, 7)
+    lower = (scaled - upper).astype(jnp.bfloat16)
+    routed = jnp.dot(
+        upper.astype(jnp.bfloat16), returned, preferred_element_type=jnp.float32
+    ) + jnp.dot(lower, returned, preferred_element_type=jnp.float32)
     mixed = (hidden + routed).astype(jnp.bfloat16)
     return mixed[None]
 

time: 425 us -> 403 us (0.948)
  local copies, waits for them, and re-layouts: 128 us -> 31.1 us
  waiting for transfers between devices: 164 us -> 240 us
    all_gather x3, waiting for transfers between devices: 23.1 us -> 90.1 us  [the longest x1 90.1 us: per_device(): lax.all_gather(down_w[0], 'exp', axis=0)]
    scatter x2 -> x0, local copies, waits for them, and re-layouts: 60.7 us -> none  [per_device(): jnp.zeros((experts, capacity, width), jnp.bfloat16).at[flat_ids, slot_of]]
    unnamed x25 -> x21, local copies, waits for them, and re-layouts: 29 us -> 9.69 us
    gather x1 -> x0, local copies, waits for them, and re-layouts: 11.5 us -> none  [per_device(): picked = returned[flat_ids, slot_of].reshape(token_count, top_k, width)]
    all_to_all x1, waiting for transfers between devices: 81.9 us -> 89.7 us  [per_device(): lax.all_to_all(cache_key_value, 'req', split_axis=1, concat_axis=0, tiled...]
    dot_general x3 -> x5, matrix products: 26.8 us -> 28.6 us  [the longest x1 16.4 us: block_terms(): jnp.einsum('krf,kdf->krd', active, down_blocks, preferred_element_type=jn...]
  transfers between devices with their start and end apart: 5 -> 5, of which waited for: 3 -> 3; matrix products, arithmetic and copies ran while one was open for 28% -> 11% of each run, Pallas kernels for 0% -> 0%
where the time goes in v1:
time: 403 us; the launch traced here: 402 us
  waiting for transfers between devices  240 us (60%)
  blocking collectives  63.6 us (16%)
  matrix products  37.1 us (9%)
  local copies, waits for them, and re-layouts  31.1 us (8%)
  between operations  14 us (3%)
  starting transfers between devices  13.3 us (3%)
    all_gather x1, waiting for transfers between devices, per_device(): lax.all_gather(down_w[0], 'exp', axis=0)  90.1 us
    all_to_all x1, waiting for transfers between devices, per_device(): lax.all_to_all(cache_key_value, 'req', split_axis=1, concat_axis=0, tiled...  89.7 us
    all_to_all x1, blocking collectives, per_device(): lax.all_to_all(outbound, 'req', split_axis=0, concat_axis=0, tiled=True)  63.6 us
    all_to_all x1, waiting for transfers between devices, per_device(): lax.all_to_all(produced, 'req', split_axis=0, concat_axis=0, tiled=True)  58.6 us
    dot_general x1, matrix products, block_terms(): jnp.einsum('krf,kdf->krd', active, down_blocks, preferred_element_type=jn...  16.4 us
    unnamed x21, local copies, waits for them, and re-layouts  9.69 us
  transfers between devices with their start and end apart: 5, of which 3 were waited for; matrix products, arithmetic and copies ran while one was open for 11% of the time, Pallas kernels for 0%

profile of v1, /device:TPU:11, one launch (start us, length us, event | category | flops | bytes accessed | tf_op | source)
XLA Modules:
  0.0 402.1 jit_solution(9093919317301286061)
XLA Ops:
  6.5 0.7 all-gather.6.cloned.1.call-update
  7.3 0.7 all-gather.4.cloned.1.call-update
  8.0 6.5 %copy.51 = bf16[128,16,1024]{2,0,1:T(8,128)(2,1)} copy(bf16[128,16,1024]{2,1,0:T(8,128)(2,1)} %param.14) | data formatting | bytes 8388608 | tf_op args[3]
  14.5 6.6 %all-to-all-start = ((bf16[128,16,1024]{2,0,1:T(8,128)(2,1)}), bf16[128,16,1024]{2,0,1:T(8,128)(2,1)}, u32[]{:S(2)}, u32[]{:S(2)}) async-start(bf16[128,16,1024]{2,0,1:T(8,128)(2,1)} %copy.51), calls=%async_computation | async-start | bytes 8388608 | tf_op jit(solution)/shard_map/all_to_all | solution.py:38
  21.1 0.2 all-gather.8.cloned.1.call-start
  21.3 0.5 all-gather.8.cloned.1.call-update
  22.5 0.4 reshape_squeeze.3
  23.4 0.4 fusion.51
  23.8 89.7 %all-to-all-done = bf16[128,16,1024]{2,0,1:T(8,128)(2,1)} async-done(((bf16[128,16,1024]{2,0,1:T(8,128)(2,1)}), bf16[128,16,1024]{2,0,1:T(8,128)(2,1)}, u32[]{:S(2)}, u32[]{:S(2)}) %all-to-all-start) | async-done | bytes 4194336 | tf_op jit(solution)/shard_map/all_to_all | solution.py:38
  113.5 4.6 %fusion.49 = (bf16[2048,512]{1,0:T(8,128)(2,1)}, bf16[2048,512]{1,0:T(8,128)(2,1)}) fusion(bf16[2048,1024]{1,0:T(8,128)(2,1)} %bitcast.4), kind=kLoop, calls=%fused_computation.74 | loop fusion | bytes 8388608 | tf_op jit(solution)/shard_map/slice | solution.py:46
  118.1 3.1 copy.52
  121.3 1.7 bitcast_reduce_fusion
  123.1 2.2 fusion.1
  125.3 2.6 copy-done
  128.1 2.5 copy.57
  130.6 6.1 %fusion.2 = f32[4,5,64,128]{3,2,1,0:T(8,128)S(1)} fusion(bf16[2048,4,128,1]{0,2,3,1:T(8,128)(2,1)} %bitcast.101, f32[4,2048,64,5]{1,2,3,0:T(8,128)} %copy-done, f32[4,5,64]{2,1,0:T(8,128)S(1)} %add.44, f32[4,5,64]{2,1,0:T(8,128)S(1)} %max.7, pred[2048]{0:T(1024)(128)(4,1)S(1)} %iota_compare_fusion.3), kind=kOutput, calls=%fused_computation.7 | convolution fusion | flops 684195840 | bytes 13250560 | tf_op jit(solution)/shard_map/gjtp,pgd->tgjd/dot_general | solution.py:75
  136.6 0.3 fusion.17
  137.0 0.4 copy.61
  137.9 0.2 multiply_reduce_fusion
  138.1 2.3 convolution_convert_fusion.1
  140.4 2.7 reshape.145
  143.2 63.6 %all_to_all.25 = bf16[16,30,2560]{2,1,0:T(8,128)(2,1)} all-to-all(bf16[16,30,2560]{2,1,0:T(8,128)(2,1)S(1)} %reshape.145), channel_id=1, replica_groups=mesh['req'=16,'exp'=2] {'req'}, dimensions={0} | all-to-all | bytes 4915200 | tf_op jit(solution)/shard_map/all_to_all | solution.py:100
  206.7 2.8 reshape.155
  209.6 7.9 %fusion.52 = f32[480,2,768]{2,0,1:T(8,128)} fusion(bf16[480,2560,1]{1,0,2:T(8,128)(2,1)S(1)} %reshape.155, bf16[2,2560,768]{2,1,0:T(8,128)(2,1)} %all-gather.6.cloned.1.call-done), kind=kOutput, calls=%fused_computation.77 | convolution fusion | flops 3774873600 | bytes 13271040 | tf_op jit(solution)/shard_map/rd,kdf->krf/dot_general | solution.py:17
  217.5 90.1 %all-gather.8.cloned.1.call-done = bf16[2,2560,768]{2,1,0:T(8,128)(2,1)} async-done(((bf16[1,2560,768]{2,1,0:T(8,128)(2,1)}), bf16[2,2560,768]{2,1,0:T(8,128)(2,1)}) %all-gather.8.cloned.1.call-update) | async-done | bytes 7864336 | tf_op jit(solution)/shard_map/all_gather | solution.py:106
  307.5 16.4 %fusion.11 = bf16[480,2560]{1,0:T(8,128)(2,1)} fusion(bf16[2,2560,768]{2,1,0:T(8,128)(2,1)} %all-gather.8.cloned.1.call-done, f32[480,2,768]{2,0,1:T(8,128)} %fusion.52, bf16[480,2560,1]{1,0,2:T(8,128)(2,1)S(1)} %reshape.155, bf16[2,2560,768]{2,1,0:T(8,128)(2,1)} %all-gather.4.cloned.1.call-done), kind=kOutput, calls=%fused_computation.22 | convolution fusion | flops 7557857280 | bytes 23592960 | tf_op jit(solution)/shard_map/krf,kdf->krd/dot_general | solution.py:19
  323.9 4.2 %reshape.147 = bf16[16,30,2560]{2,1,0:T(8,128)(2,1)} reshape(bf16[480,2560]{1,0:T(8,128)(2,1)} %fusion.11) | data formatting | bytes 4915200 | tf_op jit(solution)/shard_map/reshape | solution.py:108
  328.1 6.5 %all-to-all-start.2 = ((bf16[16,30,2560]{2,1,0:T(8,128)(2,1)}), bf16[16,30,2560]{2,1,0:T(8,128)(2,1)S(1)}, u32[]{:S(2)}, u32[]{:S(2)}) async-start(bf16[16,30,2560]{2,1,0:T(8,128)(2,1)} %reshape.147), calls=%async_computation.2 | async-start | bytes 5242880 | tf_op jit(solution)/shard_map/all_to_all | solution.py:109
  334.7 58.6 %all-to-all-done.2 = bf16[16,30,2560]{2,1,0:T(8,128)(2,1)S(1)} async-done(((bf16[16,30,2560]{2,1,0:T(8,128)(2,1)}), bf16[16,30,2560]{2,1,0:T(8,128)(2,1)S(1)}, u32[]{:S(2)}, u32[]{:S(2)}) %all-to-all-start.2) | async-done | bytes 2457632 | tf_op jit(solution)/shard_map/all_to_all | solution.py:109
  393.3 0.6 convolution_bitcast_fusion.1
  393.9 0.4 copy-done.3
  394.3 1.3 fusion.6
  (42 shorter events, 1.2 us)
Async XLA Ops:
  6.5 203.0 %all-gather.6.cloned.1.call-start = ((), (), s32[]{:S(2)}) async-start(), calls=%async_computation.4 | async-start | bytes 11796480 | tf_op jit(solution)/shard_map/all_gather | solution.py:105
  7.3 210.2 %all-gather.4.cloned.1.call-start = ((), (), s32[]{:S(2)}) async-start(), calls=%async_computation.3 | async-start | bytes 11796480 | tf_op jit(solution)/shard_map/all_gather | solution.py:104
  14.5 99.0 %all-to-all-start = ((bf16[128,16,1024]{2,0,1:T(8,128)(2,1)}), bf16[128,16,1024]{2,0,1:T(8,128)(2,1)}, u32[]{:S(2)}, u32[]{:S(2)}) async-start(bf16[128,16,1024]{2,0,1:T(8,128)(2,1)} %copy.51), calls=%async_computation | async-start | bytes 8388608 | tf_op jit(solution)/shard_map/all_to_all | solution.py:38
  21.0 1.4 copy-start.4
  21.0 1.8 copy-start.5
  21.1 1.9 copy-start.7
  21.1 286.5 %all-gather.8.cloned.1.call-start = ((), (), s32[]{:S(2)}) async-start(), calls=%async_computation.5 | async-start | bytes 11796480 | tf_op jit(solution)/shard_map/all_gather | solution.py:106
  123.0 4.9 %copy-start = (f32[4,2048,64,5]{1,2,3,0:T(8,128)}, f32[4,2048,64,5]{1,2,3,0:T(8,128)S(1)}, u32[]{:S(2)}) copy-start(f32[4,2048,64,5]{1,2,3,0:T(8,128)S(1)} %get-tuple-element.10) | copy-start | bytes 31457284
  123.1 5.0 %copy-start.1 = (bf16[2048,512]{1,0:T(8,128)(2,1)S(1)}, bf16[2048,512]{1,0:T(8,128)(2,1)}, u32[]{:S(2)}) copy-start(bf16[2048,512]{1,0:T(8,128)(2,1)} %get-tuple-element.6) | copy-start | bytes 6291460
  137.0 1.0 copy-start.2
  137.0 1.2 copy-start.6
  328.1 6.5 %copy-start.8 = (f32[1,64,6]{1,0,2:T(1,128)S(1)}, f32[1,64,6]{1,0,2:T(1,128)}, u32[]{:S(2)}) copy-start(f32[1,64,6]{1,0,2:T(1,128)} %param.17) | copy-start | bytes 4612
  328.1 65.2 %all-to-all-start.2 = ((bf16[16,30,2560]{2,1,0:T(8,128)(2,1)}), bf16[16,30,2560]{2,1,0:T(8,128)(2,1)S(1)}, u32[]{:S(2)}, u32[]{:S(2)}) async-start(bf16[16,30,2560]{2,1,0:T(8,128)(2,1)} %reshape.147), calls=%async_computation.2 | async-start | bytes 5242880 | tf_op jit(solution)/shard_map/all_to_all | solution.py:109
  393.3 1.0 copy-start.3
Sparse Core Ops, SparseCore 0:
  8.9 99.2 all-gather.5
  109.7 98.0 all-gather.3
  209.4 98.0 all-gather.7

commit v2 on v1

--- a/solution.py
+++ b/solution.py
@@ -8,18 +8,21 @@
 QUERY_HEADS = 20
 KEY_VALUE_HEADS = 4
 HEAD_SIZE = 128
+PARTS = 2
 
 
-def block_terms(batch_rows, gate_blocks, up_blocks, down_blocks):
+def hidden_units(batch_rows, gate_blocks, up_blocks):
     gate_val = jnp.einsum(
         "rd,kdf->krf", batch_rows, gate_blocks, preferred_element_type=jnp.float32
     )
     up_val = jnp.einsum("rd,kdf->krf", batch_rows, up_blocks, preferred_element_type=jnp.float32)
-    active = (jax.nn.silu(gate_val) * up_val).astype(jnp.bfloat16)
-    partial_value = jnp.einsum(
-        "krf,kdf->krd", active, down_blocks, preferred_element_type=jnp.float32
+    return (jax.nn.silu(gate_val) * up_val).astype(jnp.bfloat16)
+
+
+def block_term(active, down_part):
+    return jnp.einsum(
+        "rf,df->rd", active, down_part, preferred_element_type=jnp.float32
     ).astype(jnp.bfloat16)
-    return jnp.sum(partial_value.astype(jnp.float32), axis=0)
 
 
 def per_device(
@@ -86,6 +89,7 @@
     experts = lax.axis_size("req") * gate_w.shape[0]
     top_k = expert_ids.shape[2]
     capacity = min(token_count, 5 * token_count * top_k // (4 * experts))
+    capacity = -(-capacity // 8) * 8
     chosen = expert_ids[0][:, :, None] == jnp.arange(experts, dtype=jnp.int32)
     named = jnp.any(chosen, axis=1)
     weight = jnp.sum(jnp.where(chosen, router_w[0][:, :, None], 0.0), axis=1)
@@ -99,21 +103,43 @@
     outbound = outbound.astype(jnp.bfloat16).reshape(experts, capacity, width)
     inbound = lax.all_to_all(outbound, "req", split_axis=0, concat_axis=0, tiled=True)
     batch_rows = inbound.reshape(-1, width)
-    produced = block_terms(
-        batch_rows,
-        lax.all_gather(gate_w[0], "exp", axis=0),
-        lax.all_gather(up_w[0], "exp", axis=0),
-        lax.all_gather(down_w[0], "exp", axis=0),
+    active = hidden_units(
+        batch_rows, lax.all_gather(gate_w[0], "exp", axis=0), lax.all_gather(up_w[0], "exp", axis=0)
     )
-    produced = produced.astype(jnp.bfloat16).reshape(inbound.shape)
-    returned = lax.all_to_all(produced, "req", split_axis=0, concat_axis=0, tiled=True)
-    returned = returned.reshape(experts * capacity, width)
+    sharers = lax.axis_size("exp")
+    place_in_exp = lax.axis_index("exp")
+    own = lax.dynamic_index_in_dim(active, place_in_exp, 0, keepdims=False)
+    guests = []
+    for shift in range(1, sharers):
+        other = lax.rem(place_in_exp + shift, sharers)
+        sent = lax.dynamic_index_in_dim(active, other, 0, keepdims=False)
+        there = [(i, (i + shift) % sharers) for i in range(sharers)]
+        guests.append(lax.ppermute(sent, "exp", there))
     scaled = jnp.where(held, jnp.repeat(weight, capacity, axis=1), 0.0)
     upper = lax.reduce_precision(scaled, 8, 7)
     lower = (scaled - upper).astype(jnp.bfloat16)
-    routed = jnp.dot(
-        upper.astype(jnp.bfloat16), returned, preferred_element_type=jnp.float32
-    ) + jnp.dot(lower, returned, preferred_element_type=jnp.float32)
+    upper = upper.astype(jnp.bfloat16)
+    part = width // PARTS
+    last = None
+    routed = []
+    for piece in range(PARTS):
+        down_part = down_w[0, piece * part : (piece + 1) * part]
+        total = block_term(own, down_part).astype(jnp.float32)
+        for shift in range(1, sharers):
+            term = block_term(guests[shift - 1], down_part)
+            if last is not None:
+                term, last = lax.optimization_barrier((term, last))
+            back = [(i, (i - shift) % sharers) for i in range(sharers)]
+            last = lax.ppermute(term, "exp", back)
+            total = total + last.astype(jnp.float32)
+        produced = total.astype(jnp.bfloat16).reshape(experts, capacity, part)
+        returned = lax.all_to_all(produced, "req", split_axis=0, concat_axis=0, tiled=True)
+        returned = returned.reshape(experts * capacity, part)
+        routed.append(
+            jnp.dot(upper, returned, preferred_element_type=jnp.float32)
+            + jnp.dot(lower, returned, preferred_element_type=jnp.float32)
+        )
+    routed = jnp.concatenate(routed, axis=1)
     mixed = (hidden + routed).astype(jnp.bfloat16)
     return mixed[None]
 

time: 403 us -> 362 us (0.90)
  blocking collectives: 63.6 us -> 0 us
  starting transfers between devices: 13.3 us -> 28 us
  waiting for transfers between devices: 240 us -> 253 us
  local copies, waits for them, and re-layouts: 31.1 us -> 21.9 us
    all_gather x1 -> x0, waiting for transfers between devices: 90.1 us -> none  [per_device(): lax.all_gather(down_w[0], 'exp', axis=0)]
    ppermute x0 -> x3, waiting for transfers between devices: none -> 74 us  [the longest x2 56 us: per_device(): last = lax.ppermute(term, 'exp', back)]
    all_to_all x1 -> x0, blocking collectives: 63.6 us -> none  [per_device(): lax.all_to_all(outbound, 'req', split_axis=0, concat_axis=0, tiled=True)]
    all_to_all x0 -> x1, waiting for transfers between devices: none -> 59 us  [per_device(): lax.all_to_all(outbound, 'req', split_axis=0, concat_axis=0, tiled=True)]
    all_to_all x1 -> x2, waiting for transfers between devices: 58.6 us -> 29 us  [per_device(): lax.all_to_all(produced, 'req', split_axis=0, concat_axis=0, tiled=True)]
    reshape x3 -> x0, local copies, waits for them, and re-layouts: 9.71 us -> none  [the longest x1 4.21 us: per_device(): produced = produced.astype(jnp.bfloat16).reshape(inbound.shape)]
    all_to_all x1 -> x2, starting transfers between devices: 6.5 us -> 12.5 us  [per_device(): lax.all_to_all(produced, 'req', split_axis=0, concat_axis=0, tiled=True)]
    all_to_all x0 -> x1, starting transfers between devices: none -> 4.84 us  [per_device(): lax.all_to_all(outbound, 'req', split_axis=0, concat_axis=0, tiled=True)]
  transfers between devices with their start and end apart: 5 -> 9, of which waited for: 3 -> 6; matrix products, arithmetic and copies ran while one was open for 11% -> 13% of each run, Pallas kernels for 0% -> 0%
where the time goes in v2:
time: 362 us
  waiting for transfers between devices  253 us (70%)
  matrix products  39.5 us (11%)
  starting transfers between devices  28 us (8%)
  local copies, waits for them, and re-layouts  21.9 us (6%)
  between operations  14.4 us (4%)
  other arithmetic  4.95 us (1%)
    all_to_all x1, waiting for transfers between devices, per_device(): lax.all_to_all(cache_key_value, 'req', split_axis=1, concat_axis=0, tiled...  89.7 us
    all_to_all x1, waiting for transfers between devices, per_device(): lax.all_to_all(outbound, 'req', split_axis=0, concat_axis=0, tiled=True)  59 us
    ppermute x2, waiting for transfers between devices, per_device(): last = lax.ppermute(term, 'exp', back)  56 us
    all_to_all x2, waiting for transfers between devices, per_device(): lax.all_to_all(produced, 'req', split_axis=0, concat_axis=0, tiled=True)  29 us
    ppermute x1, waiting for transfers between devices, per_device(): guests.append(lax.ppermute(sent, 'exp', there))  18 us
    all_to_all x2, starting transfers between devices, per_device(): lax.all_to_all(produced, 'req', split_axis=0, concat_axis=0, tiled=True)  12.5 us
    unnamed x33, local copies, waits for them, and re-layouts  10.3 us
    dot_general x4, matrix products, block_term(): jnp.einsum('rf,df->rd', active, down_part, preferred_element_type=jnp.flo...  9.66 us
  transfers between devices with their start and end apart: 9, of which 6 were waited for; matrix products, arithmetic and copies ran while one was open for 13% of the time, Pallas kernels for 0%

profile of v2, /device:TPU:11, one launch (start us, length us, event | category | flops | bytes accessed | tf_op | source)
XLA Modules:
  0.0 361.8 jit_solution(15710934293051493812)
XLA Ops:
  7.3 6.5 %copy.51 = bf16[128,16,1024]{2,0,1:T(8,128)(2,1)} copy(bf16[128,16,1024]{2,1,0:T(8,128)(2,1)} %param.14) | data formatting | bytes 8388608 | tf_op args[3]
  13.7 6.6 %all-to-all-start = ((bf16[128,16,1024]{2,0,1:T(8,128)(2,1)}), bf16[128,16,1024]{2,0,1:T(8,128)(2,1)}, u32[]{:S(2)}, u32[]{:S(2)}) async-start(bf16[128,16,1024]{2,0,1:T(8,128)(2,1)} %copy.51), calls=%async_computation | async-start | bytes 8388608 | tf_op jit(solution)/shard_map/all_to_all | solution.py:41
  23.0 89.7 %all-to-all-done = bf16[128,16,1024]{2,0,1:T(8,128)(2,1)} async-done(((bf16[128,16,1024]{2,0,1:T(8,128)(2,1)}), bf16[128,16,1024]{2,0,1:T(8,128)(2,1)}, u32[]{:S(2)}, u32[]{:S(2)}) %all-to-all-start) | async-done | bytes 4194336 | tf_op jit(solution)/shard_map/all_to_all | solution.py:41
  112.7 4.6 %fusion.69 = (bf16[2048,512]{1,0:T(8,128)(2,1)}, bf16[2048,512]{1,0:T(8,128)(2,1)}) fusion(bf16[2048,1024]{1,0:T(8,128)(2,1)} %bitcast.3), kind=kLoop, calls=%fused_computation.98 | loop fusion | bytes 8388608 | tf_op jit(solution)/shard_map/slice | solution.py:49
  117.4 3.1 copy.52
  120.5 1.7 bitcast_reduce_fusion
  122.3 2.2 fusion.1
  124.5 2.7 copy-done
  127.4 2.5 copy.57
  129.8 6.1 %fusion.2 = f32[4,5,64,128]{3,2,1,0:T(8,128)S(1)} fusion(bf16[2048,4,128,1]{0,2,3,1:T(8,128)(2,1)} %bitcast.133, f32[4,2048,64,5]{1,2,3,0:T(8,128)} %copy-done, f32[4,5,64]{2,1,0:T(8,128)S(1)} %add.65, f32[4,5,64]{2,1,0:T(8,128)S(1)} %max.7, pred[2048]{0:T(1024)(128)(4,1)S(1)} %iota_compare_fusion.3), kind=kOutput, calls=%fused_computation.6 | convolution fusion | flops 684195840 | bytes 13250560 | tf_op jit(solution)/shard_map/gjtp,pgd->tgjd/dot_general | solution.py:78
  137.4 2.4 convolution_convert_fusion
  139.8 4.8 %all-to-all-start.1 = ((bf16[16,32,2560]{2,1,0:T(8,128)(2,1)}), bf16[16,32,2560]{2,1,0:T(8,128)(2,1)S(1)}, u32[]{:S(2)}, u32[]{:S(2)}) async-start(bf16[16,32,2560]{2,1,0:T(8,128)(2,1)} %bitcast.19), calls=%async_computation.1 | async-start | bytes 5242880 | tf_op jit(solution)/shard_map/all_to_all | solution.py:104
  144.7 59.0 %all-to-all-done.1 = bf16[16,32,2560]{2,1,0:T(8,128)(2,1)S(1)} async-done(((bf16[16,32,2560]{2,1,0:T(8,128)(2,1)}), bf16[16,32,2560]{2,1,0:T(8,128)(2,1)S(1)}, u32[]{:S(2)}, u32[]{:S(2)}) %all-to-all-start.1) | async-done | bytes 2621472 | tf_op jit(solution)/shard_map/all_to_all | solution.py:104
  203.7 8.2 %fusion.72 = f32[512,2,768]{2,0,1:T(8,128)} fusion(bf16[512,2560,1]{1,0,2:T(8,128)(2,1)S(1)} %bitcast.131, bf16[2,2560,768]{2,1,0:T(8,128)(2,1)} %all-gather.5.cloned.1.call-done), kind=kOutput, calls=%fused_computation.101 | convolution fusion | flops 4026531840 | bytes 13631488 | tf_op jit(solution)/shard_map/rd,kdf->krf/dot_general | solution.py:18
  211.9 8.5 %fusion.3 = bf16[2,512,768]{2,1,0:T(8,128)(2,1)S(1)} fusion(f32[512,2,768]{2,0,1:T(8,128)} %fusion.72, bf16[512,2560,1]{1,0,2:T(8,128)(2,1)S(1)} %bitcast.132, bf16[2,2560,768]{2,1,0:T(8,128)(2,1)} %all-gather.3.cloned.1.call-done), kind=kOutput, calls=%fused_computation.9 | convolution fusion | flops 4031250432 | bytes 15204352 | tf_op jit(solution)/shard_map/rd,kdf->krf/dot_general | solution.py:15
  220.5 1.3 collective-permute-start
  221.8 18.0 %collective-permute-done = bf16[512,768]{1,0:T(8,128)(2,1)S(1)} collective-permute-done((bf16[512,768]{1,0:T(8,128)(2,1)S(1)}, bf16[512,768]{1,0:T(8,128)(2,1)S(1)}, u32[]{:S(2)}, u32[]{:S(2)}) %collective-permute-start) | collective-permute-done | bytes 786464 | tf_op jit(solution)/shard_map/ppermute | solution.py:117
  239.8 0.9 copy-done.14
  240.7 1.2 convolution_convert_fusion.3
  242.0 1.3 collective-permute-start.1
  243.3 28.4 %collective-permute-done.1 = bf16[512,1280]{1,0:T(8,128)(2,1)S(1)} collective-permute-done((bf16[512,1280]{1,0:T(8,128)(2,1)S(1)}, bf16[512,1280]{1,0:T(8,128)(2,1)S(1)}, u32[]{:S(2)}, u32[]{:S(2)}) %collective-permute-start.1) | collective-permute-done | bytes 1310752 | tf_op jit(solution)/shard_map/ppermute | solution.py:133
  271.7 4.1 %add_convert_fusion.1 = bf16[512,1280]{1,0:T(8,128)(2,1)} fusion(bf16[512,1280]{1,0:T(8,128)(2,1)S(1)} %collective-permute-done.1, bf16[1,2560,768]{2,1,0:T(8,128)(2,1)} %param.21, bf16[2,512,768]{2,1,0:T(8,128)(2,1)} %copy-done.5, s32[]{:T(128)S(6)} %select_n.35), kind=kOutput, calls=%fused_computation.22 | convolution fusion | flops 1009909760 | bytes 5373956 | tf_op jit(solution)/shard_map/rf,df->rd/dot_general | solution.py:23
  275.7 5.5 %all-to-all-start.2 = ((bf16[16,32,1280]{2,1,0:T(8,128)(2,1)}), bf16[16,32,1280]{2,1,0:T(8,128)(2,1)S(1)}, u32[]{:S(2)}, u32[]{:S(2)}) async-start(bf16[16,32,1280]{2,1,0:T(8,128)(2,1)} %bitcast.28), calls=%async_computation.2 | async-start | bytes 2621440 | tf_op jit(solution)/shard_map/all_to_all | solution.py:136
  281.2 3.1 convolution_convert_fusion.1
  284.4 1.3 collective-permute-start.2
  285.7 1.2 fusion.8
  286.9 27.5 %collective-permute-done.2 = bf16[512,1280]{1,0:T(8,128)(2,1)S(1)} collective-permute-done((bf16[512,1280]{1,0:T(8,128)(2,1)S(1)}, bf16[512,1280]{1,0:T(8,128)(2,1)S(1)}, u32[]{:S(2)}, u32[]{:S(2)}) %collective-permute-start.2) | collective-permute-done | bytes 1310752 | tf_op jit(solution)/shard_map/ppermute | solution.py:133
  314.5 1.4 add_convert_fusion
  315.8 7.0 %all-to-all-start.3 = ((bf16[16,32,1280]{2,1,0:T(8,128)(2,1)}), bf16[16,32,1280]{2,1,0:T(8,128)(2,1)S(1)}, u32[]{:S(2)}, u32[]{:S(2)}) async-start(bf16[16,32,1280]{2,1,0:T(8,128)(2,1)} %bitcast.130), calls=%async_computation.3 | async-start | bytes 2621440 | tf_op jit(solution)/shard_map/all_to_all | solution.py:136
  323.2 1.1 fusion.12
  324.4 29.0 %all-to-all-done.3 = bf16[16,32,1280]{2,1,0:T(8,128)(2,1)S(1)} async-done(((bf16[16,32,1280]{2,1,0:T(8,128)(2,1)}), bf16[16,32,1280]{2,1,0:T(8,128)(2,1)S(1)}, u32[]{:S(2)}, u32[]{:S(2)}) %all-to-all-start.3) | async-done | bytes 1310752 | tf_op jit(solution)/shard_map/all_to_all | solution.py:136
  354.2 0.8 fusion.35
  (65 shorter events, 5.6 us)
Async XLA Ops:
  6.5 138.1 %all-gather.5.cloned.1.call-start = ((), (), s32[]{:S(2)}) async-start(), calls=%async_computation.5 | async-start | bytes 11796480 | tf_op jit(solution)/shard_map/all_gather | solution.py:107
  13.7 99.0 %all-to-all-start = ((bf16[128,16,1024]{2,0,1:T(8,128)(2,1)}), bf16[128,16,1024]{2,0,1:T(8,128)(2,1)}, u32[]{:S(2)}, u32[]{:S(2)}) async-start(bf16[128,16,1024]{2,0,1:T(8,128)(2,1)} %copy.51), calls=%async_computation | async-start | bytes 8388608 | tf_op jit(solution)/shard_map/all_to_all | solution.py:41
  20.3 1.4 copy-start.7
  20.3 1.9 copy-start.8
  20.3 1.9 copy-start.10
  20.3 191.6 %all-gather.3.cloned.1.call-start = ((), (), s32[]{:S(2)}) async-start(), calls=%async_computation.4 | async-start | bytes 11796480 | tf_op jit(solution)/shard_map/all_gather | solution.py:107
  122.3 5.0 %copy-start = (f32[4,2048,64,5]{1,2,3,0:T(8,128)}, f32[4,2048,64,5]{1,2,3,0:T(8,128)S(1)}, u32[]{:S(2)}) copy-start(f32[4,2048,64,5]{1,2,3,0:T(8,128)S(1)} %get-tuple-element.12) | copy-start | bytes 31457284
  122.3 5.1 %copy-start.1 = (bf16[2048,512]{1,0:T(8,128)(2,1)S(1)}, bf16[2048,512]{1,0:T(8,128)(2,1)}, u32[]{:S(2)}) copy-start(bf16[2048,512]{1,0:T(8,128)(2,1)} %get-tuple-element.8) | copy-start | bytes 6291460
  136.2 1.0 copy-start.2
  136.6 0.8 copy-start.9
  139.8 63.9 %all-to-all-start.1 = ((bf16[16,32,2560]{2,1,0:T(8,128)(2,1)}), bf16[16,32,2560]{2,1,0:T(8,128)(2,1)S(1)}, u32[]{:S(2)}, u32[]{:S(2)}) async-start(bf16[16,32,2560]{2,1,0:T(8,128)(2,1)} %bitcast.19), calls=%async_computation.1 | async-start | bytes 5242880 | tf_op jit(solution)/shard_map/all_to_all | solution.py:104
  211.9 28.8 %copy-start.12 = (bf16[1,2560,768]{2,1,0:T(8,128)(2,1)S(1)}, bf16[1,2560,768]{2,1,0:T(8,128)(2,1)}, u32[]{:S(2)}) copy-start(bf16[1,2560,768]{2,1,0:T(8,128)(2,1)} %param.21) | copy-start | bytes 11796484
  220.4 21.6 %copy-start.5 = (bf16[2,512,768]{2,1,0:T(8,128)(2,1)}, bf16[2,512,768]{2,1,0:T(8,128)(2,1)S(1)}, u32[]{:S(2)}) copy-start(bf16[2,512,768]{2,1,0:T(8,128)(2,1)S(1)} %fusion.3) | copy-start | bytes 4718596
  220.5 19.4 %collective-permute-start = (bf16[512,768]{1,0:T(8,128)(2,1)S(1)}, bf16[512,768]{1,0:T(8,128)(2,1)S(1)}, u32[]{:S(2)}, u32[]{:S(2)}) collective-permute-start(bf16[512,768]{1,0:T(8,128)(2,1)S(1)} %dynamic-slice_bitcast_fusion), channel_id=1, source_target_pairs={{0,1},{1,0},{2,3},{3,2},{4,5},{5,4},{6,7},{7,6},{8,9},{9,8},{10,11... | collective-permute-start | bytes 2359304 | tf_op jit(solution)/shard_map/ppermute | solution.py:117
  239.8 0.9 copy-start.14
  242.0 29.7 %collective-permute-start.1 = (bf16[512,1280]{1,0:T(8,128)(2,1)S(1)}, bf16[512,1280]{1,0:T(8,128)(2,1)S(1)}, u32[]{:S(2)}, u32[]{:S(2)}) collective-permute-start(bf16[512,1280]{1,0:T(8,128)(2,1)S(1)} %convolution_convert_fusion.3), channel_id=1, source_target_pairs={{0,1},{1,0},{2,3},{3,2},{4,5},{5,4},{6,7},{7,6},{8,9},{9,8},{10,11... | collective-permute-start | bytes 3932168 | tf_op jit(solution)/shard_map/ppermute | solution.py:133
  275.7 40.1 %all-to-all-start.2 = ((bf16[16,32,1280]{2,1,0:T(8,128)(2,1)}), bf16[16,32,1280]{2,1,0:T(8,128)(2,1)S(1)}, u32[]{:S(2)}, u32[]{:S(2)}) async-start(bf16[16,32,1280]{2,1,0:T(8,128)(2,1)} %bitcast.28), calls=%async_computation.2 | async-start | bytes 2621440 | tf_op jit(solution)/shard_map/all_to_all | solution.py:136
  281.2 4.5 %copy-start.6 = (bf16[2,512,768]{2,1,0:T(8,128)(2,1)S(1)}, bf16[2,512,768]{2,1,0:T(8,128)(2,1)}, u32[]{:S(2)}) copy-start(bf16[2,512,768]{2,1,0:T(8,128)(2,1)} %copy-done.5) | copy-start | bytes 4718596
  281.2 4.5 %copy-start.13 = (bf16[1,2560,768]{2,1,0:T(8,128)(2,1)S(1)}, bf16[1,2560,768]{2,1,0:T(8,128)(2,1)}, u32[]{:S(2)}) copy-start(bf16[1,2560,768]{2,1,0:T(8,128)(2,1)} %param.21) | copy-start | bytes 11796484
  284.4 30.1 %collective-permute-start.2 = (bf16[512,1280]{1,0:T(8,128)(2,1)S(1)}, bf16[512,1280]{1,0:T(8,128)(2,1)S(1)}, u32[]{:S(2)}, u32[]{:S(2)}) collective-permute-start(bf16[512,1280]{1,0:T(8,128)(2,1)S(1)} %convolution_convert_fusion.1), channel_id=1, source_target_pairs={{0,1},{1,0},{2,3},{3,2},{4,5},{5,4},{6,7},{7,6},{8,9},{9,8},{10,11... | collective-permute-start | bytes 3932168 | tf_op jit(solution)/shard_map/ppermute | solution.py:133
  315.8 7.0 %copy-start.11 = (f32[1,64,6]{1,0,2:T(1,128)S(1)}, f32[1,64,6]{1,0,2:T(1,128)}, u32[]{:S(2)}) copy-start(f32[1,64,6]{1,0,2:T(1,128)} %param.17) | copy-start | bytes 4612
  315.8 37.5 %all-to-all-start.3 = ((bf16[16,32,1280]{2,1,0:T(8,128)(2,1)}), bf16[16,32,1280]{2,1,0:T(8,128)(2,1)S(1)}, u32[]{:S(2)}, u32[]{:S(2)}) async-start(bf16[16,32,1280]{2,1,0:T(8,128)(2,1)} %bitcast.130), calls=%async_computation.3 | async-start | bytes 2621440 | tf_op jit(solution)/shard_map/all_to_all | solution.py:136
  324.4 29.8 %copy-start.3 = (bf16[1,64,2560]{2,1,0:T(8,128)(2,1)S(1)}, bf16[1,64,2560]{2,1,0:T(8,128)(2,1)}, u32[]{:S(2)}) copy-start(bf16[1,64,2560]{2,1,0:T(8,128)(2,1)} %param.11) | copy-start | bytes 983044
  324.4 29.8 %copy-start.4 = (f32[1,64,1280]{2,1,0:T(8,128)S(1)}, f32[1,64,1280]{2,1,0:T(8,128)}, u32[]{:S(2)}) copy-start(f32[1,64,1280]{2,1,0:T(8,128)} %fusion.12) | copy-start | bytes 983044
Sparse Core Ops, SparseCore 0:
  8.9 99.2 all-gather.4
  109.7 98.0 all-gather.2
